TPU v7x, 256 devices: a whole 4x4x8 slice. The times are simulated.
256 devices in a mesh: seq: 32 (over y, z), mp: 8 (over x, core).
Axes of the slice: x: 4, y: 4, z: 8, core: 2. Of those that a mesh axis runs over, the one named last changes fastest.
Arguments:
- patch_hidden: bfloat16 [16384, 5120], P('seq', 'mp'), may hold values from -6 to 6
- out_weight: bfloat16 [5120, 8192], P(None, 'mp'), may hold values from -0.078125 to 0.078125
- out_bias: bfloat16 [8192], P('mp'), may hold values from -3 to 3
- cluster_ids: int32 [16384], P('seq'), may hold values from 0 to 8191, as said below
- memory_slots: bfloat16 [8192, 8192], P('seq', 'mp'), may hold values from -6 to 6
- slot_counts: int32 [8192], P('seq'), may hold values from 1 to 16
- norm_gain: bfloat16 [8192], P('mp'), may hold values from 0.099609375 to 1.8984375
- key_weight: bfloat16 [8192, 1024], P('seq', 'mp'), may hold values from -0.0625 to 0.0625
- value_weight: bfloat16 [8192, 1024], P('seq', 'mp'), may hold values from -0.0625 to 0.0625
- key_bias: bfloat16 [1024], P('mp'), may hold values from -3 to 3
- value_bias: bfloat16 [1024], P('mp'), may hold values from -3 to 3
Outputs:
- memory_new: bfloat16 [8192, 8192], P('seq', 'mp')
- slot_keys: bfloat16 [8192, 1024], P('seq', 'mp')
- slot_values: bfloat16 [8192, 1024], P('seq', 'mp')
Inputs may be any that keep to these rules, and one draw needn't show every extreme that they name: `cluster_ids`: slots s * 256 to (s + 1) * 256 - 1 belong to index s of seq. Of the 512 rows of one index of seq, at most 48 name slots of any one index of seq, and in every draw some index of seq receives exactly 48 rows from every index of seq.
All inputs are finite; a program needn't handle non-finite values.
Results may differ from a plain program's by a relative error of at most 0.0054.
Values may be sent and summed in bfloat16 or wider, within the bound.
A program may use at most 128 MiB of HBM per device.

v0:
```python
import jax
import jax.numpy as jnp
from jax import lax
from jax.sharding import PartitionSpec as P

D = 8192


def on_device(
    patch_hidden,
    out_weight,
    out_bias,
    cluster_ids,
    memory_slots,
    slot_counts,
    norm_gain,
    key_weight,
    value_weight,
    key_bias,
    value_bias,
):
    row_count = patch_hidden.shape[0]
    width_local = out_weight.shape[1]
    slot_local = memory_slots.shape[0]
    seq_count = lax.axis_size("seq")
    capacity = 3 * row_count // seq_count
    bias_wide = out_bias.astype(jnp.float32)
    owner = cluster_ids // slot_local
    owner_table = (owner[:, None] == jnp.arange(seq_count, dtype=jnp.int32)[None, :]).astype(
        jnp.int32
    )
    rank = jnp.sum(jnp.cumsum(owner_table, axis=0) * owner_table, axis=1) - 1
    target = owner * capacity + rank
    send_slots = (
        jnp.full((seq_count * capacity,), -1, jnp.int32).at[target].set(cluster_ids % slot_local)
    )
    activated = jax.nn.gelu(
        lax.all_gather(patch_hidden, "mp", axis=1, tiled=True).astype(jnp.float32),
        approximate=False,
    ).astype(jnp.bfloat16)
    projected = jnp.dot(activated, out_weight, preferred_element_type=jnp.float32)
    merged = projected + bias_wide[None, :]
    send_rows = jnp.zeros((seq_count * capacity, width_local), jnp.float32).at[target].set(merged)
    got_rows, got_slots = (
        lax.all_to_all(send_rows, "seq", split_axis=0, concat_axis=0, tiled=True),
        lax.all_to_all(send_slots, "seq", split_axis=0, concat_axis=0, tiled=True),
    )
    matches = jnp.arange(slot_local, dtype=jnp.int32)[:, None] == got_slots[None, :]
    totals = jnp.dot(
        matches.astype(jnp.float32),
        got_rows,
        precision=lax.Precision.HIGHEST,
        preferred_element_type=jnp.float32,
    )
    arrivals = jnp.sum(matches.astype(jnp.float32), axis=1)
    weight = slot_counts.astype(jnp.float32)
    memory_new = (
        (weight[:, None] * memory_slots.astype(jnp.float32) + totals) / (weight + arrivals)[:, None]
    ).astype(jnp.bfloat16)
    key_full, value_full = (
        lax.all_gather(key_weight, "seq", axis=0, tiled=True),
        lax.all_gather(value_weight, "seq", axis=0, tiled=True),
    )
    head_local = key_full.shape[1]
    stored = lax.optimization_barrier(memory_new).astype(jnp.float32)
    squares = lax.psum(jnp.sum(stored * stored, axis=1), "mp")
    inverse = lax.rsqrt(squares / D + 1e-06)
    normed = (stored * inverse[:, None] * norm_gain.astype(jnp.float32)[None, :]).astype(
        jnp.bfloat16
    )
    key_rows, value_rows = (
        lax.all_to_all(key_full, "mp", split_axis=0, concat_axis=1, tiled=True),
        lax.all_to_all(value_full, "mp", split_axis=0, concat_axis=1, tiled=True),
    )
    mp_count = key_rows.shape[1] // head_local
    joined = jnp.stack(
        [
            key_rows.reshape(width_local, mp_count, head_local),
            value_rows.reshape(width_local, mp_count, head_local),
        ],
        axis=2,
    ).reshape(width_local, 2 * mp_count * head_local)
    shared = lax.psum_scatter(
        lax.dot_general(
            joined, normed, (((0,), (1,)), ((), ())), preferred_element_type=jnp.float32
        ),
        "mp",
        scatter_dimension=0,
        tiled=True,
    )
    combined = shared.T
    key_part = combined[:, :head_local]
    value_part = combined[:, head_local:]
    slot_keys = (key_part + key_bias.astype(jnp.float32)[None, :]).astype(jnp.bfloat16)
    slot_values = (value_part + value_bias.astype(jnp.float32)[None, :]).astype(jnp.bfloat16)
    return (memory_new, slot_keys, slot_values)


def solution(mesh):
    return jax.shard_map(
        on_device,
        mesh=mesh,
        in_specs=(
            P("seq", "mp"),
            P(None, "mp"),
            P("mp"),
            P("seq"),
            P("seq", "mp"),
            P("seq"),
            P("mp"),
            P("seq", "mp"),
            P("seq", "mp"),
            P("mp"),
            P("mp"),
        ),
        out_specs=(P("seq", "mp"), P("seq", "mp"), P("seq", "mp")),
        check_vma=False,
    )
```

profile of v0, /device:TPU:8, one launch (start us, length us, event | category | flops | bytes accessed | tf_op | source)
XLA Modules:
  0.0 477.1 jit_solution(14380446403744334530)
XLA Ops:
  7.2 0.0 all-gather.8.cloned.1.call-start
  7.2 0.7 all-gather.8.cloned.1.call-update
  7.9 0.0 all-gather.6.cloned.1.call-start
  7.9 0.7 all-gather.6.cloned.1.call-update
  8.6 0.0 all-gather.4.cloned.1.call-start
  8.7 0.7 all-gather.4.cloned.1.call-update
  9.4 0.7 add_select_fusion
  10.1 1.2 reduce-window.6
  11.3 0.2 slice_reduce_fusion
  11.5 0.1 fusion.52
  11.6 2.5 scatter_custom_fusion
  14.1 0.1 all_to_all.38
  14.2 20.1 %all_to_all.53 = s32[32,48,1]{1,2,0:T(1,128)S(1)} all-to-all(s32[32,48,1]{1,2,0:T(1,128)S(1)} %bitcast.39), channel_id=1, replica_groups=mesh['seq'=32,'mp'=8] {'seq'}, dimensions={0} | all-to-all | bytes 12288 | tf_op jit(solution)/shard_map/all_to_all | solution.py:46
  34.3 55.9 %all-gather.8.cloned.1.call-done = bf16[8192,128]{1,0:T(8,128)(2,1)} async-done(((bf16[256,128]{1,0:T(8,128)(2,1)}), bf16[8192,128]{1,0:T(8,128)(2,1)}) %all-gather.8.cloned.1.call-update) | async-done | bytes 2097168 | tf_op jit(solution)/shard_map/all_gather | solution.py:62
  90.2 4.3 all-to-all-start.3
  94.5 0.7 convert_element_type.53
  95.2 72.8 %all-gather.6.cloned.1.call-done = bf16[8192,128]{1,0:T(8,128)(2,1)} async-done(((bf16[256,128]{1,0:T(8,128)(2,1)}), bf16[8192,128]{1,0:T(8,128)(2,1)}) %all-gather.6.cloned.1.call-update) | async-done | bytes 2097168 | tf_op jit(solution)/shard_map/all_gather | solution.py:61
  168.0 0.0 all-to-all-done.3
  168.0 4.4 all-to-all-start.2
  172.3 49.5 %all-gather.4.cloned.1.call-done = bf16[512,5120]{1,0:T(8,128)(2,1)} async-done(((bf16[512,640]{1,0:T(8,128)(2,1)}), bf16[512,5120]{1,0:T(8,128)(2,1)}) %all-gather.4.cloned.1.call-update) | async-done | bytes 5242896 | tf_op jit(solution)/shard_map/all_gather | solution.py:38
  221.8 31.9 %fusion.31 = f32[512,1024]{1,0:T(8,128)} fusion(bf16[5120,1024]{1,0:T(8,128)(2,1)} %param.12, bf16[512,5120]{1,0:T(8,128)(2,1)} %all-gather.4.cloned.1.call-done), kind=kOutput, calls=%fused_computation.36 | convolution fusion | flops 5541724160 | bytes 17825792 | tf_op jit(solution)/shard_map/dot_general | solution.py:41
  253.7 0.0 copy-start.1
  253.7 0.0 copy-start.2
  253.7 6.4 %scatter_custom_fusion.1 = f32[1536,1024]{1,0:T(8,128)} fusion(s32[512]{0:T(512)S(1)} %compare_select_fusion, f32[]{:T(128)} %constant.48.clone.1, f32[512,1024]{1,0:T(8,128)} %fusion.31, f32[1024]{0:T(1024)S(1)} %convert_element_type.53), kind=kCustom, calls=%fused_computation.38 | custom fusion | flops 524288 | bytes 8392708 | tf_op jit(solution)/shard_map/scatter | solution.py:43
  260.2 0.0 all-to-all-done.2
  260.2 7.3 %all-to-all-start.1 = ((f32[32,48,1024]{2,1,0:T(8,128)}), f32[32,48,1024]{2,1,0:T(8,128)}, u32[]{:S(2)}, u32[]{:S(2)}) async-start(f32[32,48,1024]{2,1,0:T(8,128)} %bitcast.33), calls=%async_computation.1 | async-start | bytes 12582912 | tf_op jit(solution)/shard_map/all_to_all | solution.py:45
  267.5 0.0 copy-start.3
  267.5 0.0 reduce-scatter.2.cloned.1.call-start
  267.6 0.0 copy-done.1
  267.6 0.0 copy-done.2
  267.6 0.5 broadcast.74
  268.1 0.7 reduce.5
  268.8 0.1 eq.48
  268.9 0.2 convert_reduce_fusion
  269.2 3.9 pad_maximum_fusion
  273.1 6.5 %copy.30 = bf16[1024,8,2,128]{0,3,2,1:T(8,128)(2,1)} copy(bf16[1024,8,2,128]{3,0,1,2:T(8,128)(2,1)} %pad_maximum_fusion) | data formatting | bytes 8388608 | tf_op jit(solution)/shard_map/stack | solution.py:76
  279.5 0.0 copy-start.4
  279.5 0.0 copy-start.5
  279.5 128.1 %all-to-all-done.1 = f32[32,48,1024]{2,1,0:T(8,128)} async-done(((f32[32,48,1024]{2,1,0:T(8,128)}), f32[32,48,1024]{2,1,0:T(8,128)}, u32[]{:S(2)}, u32[]{:S(2)}) %all-to-all-start.1) | async-done | bytes 6291488 | tf_op jit(solution)/shard_map/all_to_all | solution.py:45
  407.6 0.0 copy-done.3
  407.6 6.3 %fusion.39 = bf16[256,1024]{1,0:T(8,128)(2,1)S(1)} fusion(f32[1536,1024]{1,0:T(8,128)} %bitcast.4, bf16[256,1024]{1,0:T(8,128)(2,1)S(1)} %copy-done.3, s32[1536]{0:T(1024)S(1)} %eq.48, f32[256]{0:T(256)S(1)} %convert_add_fusion, f32[256]{0:T(256)S(1)} %convert_element_type.48), kind=kOutput, calls=%fused_computation.48 | convolution fusion | flops 4833542144 | bytes 7348224 | tf_op jit(solution)/shard_map/dot_general | solution.py:49
  413.9 0.0 copy-start
  413.9 0.2 fusion.40
  414.1 12.4 %psum.7 = f32[256]{0:T(256)S(1)} all-reduce(f32[256]{0:T(256)S(1)} %fusion.40), channel_id=1, replica_groups=mesh['seq'=32,'mp'=8] {'mp'}, use_global_device_ids=true, to_apply=%region_7.8 | all-reduce | flops 256 | bytes 2048 | tf_op jit(solution)/shard_map/psum | solution.py:66
  426.5 4.9 %fusion.45 = f32[2048,256]{1,0:T(8,128)} fusion(bf16[1024,2048]{0,1:T(8,128)(2,1)} %bitcast.35, bf16[256,1024]{1,0:T(8,128)(2,1)S(1)} %fusion.39, f32[1024]{0:T(1024)S(1)} %convert_element_type.57, f32[256]{0:T(256)S(1)} %add_rsqrt_fusion), kind=kOutput, calls=%fused_computation.54 | convolution fusion | flops 1074790400 | bytes 6820864 | tf_op jit(solution)/shard_map/dot_general | solution.py:84
  431.4 0.0 reduce-scatter.2.cloned.1.call-update
  431.4 0.0 copy-done.4
  431.5 0.0 copy-done.5
  431.5 36.5 %reduce-scatter.2.cloned.1.call-done = f32[256,256]{1,0:T(8,128)} async-done(((f32[2048,256]{1,0:T(8,128)}), f32[256,256]{1,0:T(8,128)}) %reduce-scatter.2.cloned.1.call-update) | async-done | bytes 262160 | tf_op jit(solution)/shard_map/reduce_scatter | solution.py:83
  468.0 1.1 fusion.49
  469.1 0.7 copy.31
  469.8 0.7 copy.32
  470.6 0.0 copy-done
  (10 shorter events, 0.1 us)
Async XLA Ops:
  7.2 83.1 %all-gather.8.cloned.1.call-start = ((), (), s32[]{:S(2)}) async-start(), calls=%async_computation.7 | async-start | bytes 2162688 | tf_op jit(solution)/shard_map/all_gather | solution.py:62
  7.9 160.1 %all-gather.6.cloned.1.call-start = ((), (), s32[]{:S(2)}) async-start(), calls=%async_computation.6 | async-start | bytes 2162688 | tf_op jit(solution)/shard_map/all_gather | solution.py:61
  8.6 213.2 %all-gather.4.cloned.1.call-start = ((), (), s32[]{:S(2)}) async-start(), calls=%async_computation.5 | async-start | bytes 5898240 | tf_op jit(solution)/shard_map/all_gather | solution.py:38
  90.2 77.7 %all-to-all-start.3 = ((bf16[8,1024,128]{2,1,0:T(8,128)(2,1)}), bf16[8,1024,128]{2,1,0:T(8,128)(2,1)S(1)}, u32[]{:S(2)}, u32[]{:S(2)}) async-start(bf16[8,1024,128]{2,1,0:T(8,128)(2,1)} %bitcast.37), calls=%async_computation.3 | async-start | bytes 4194304 | tf_op jit(solution)/shard_map/all_to_all | solution.py:73
  168.0 92.2 %all-to-all-start.2 = ((bf16[8,1024,128]{2,1,0:T(8,128)(2,1)}), bf16[8,1024,128]{2,1,0:T(8,128)(2,1)}, u32[]{:S(2)}, u32[]{:S(2)}) async-start(bf16[8,1024,128]{2,1,0:T(8,128)(2,1)} %bitcast.36), calls=%async_computation.2 | async-start | bytes 4194304 | tf_op jit(solution)/shard_map/all_to_all | solution.py:72
  253.7 13.9 %copy-start.1 = (s32[256]{0:T(256)S(1)}, s32[256]{0:T(256)}, u32[]{:S(2)}) copy-start(s32[256]{0:T(256)} %param.16) | copy-start | bytes 3076
  253.7 13.9 %copy-start.2 = (bf16[1024]{0:T(1024)(128)(2,1)S(1)}, bf16[1024]{0:T(1024)(128)(2,1)}, u32[]{:S(2)}) copy-start(bf16[1024]{0:T(1024)(128)(2,1)} %param.17) | copy-start | bytes 6148
  260.2 147.4 %all-to-all-start.1 = ((f32[32,48,1024]{2,1,0:T(8,128)}), f32[32,48,1024]{2,1,0:T(8,128)}, u32[]{:S(2)}, u32[]{:S(2)}) async-start(f32[32,48,1024]{2,1,0:T(8,128)} %bitcast.33), calls=%async_computation.1 | async-start | bytes 12582912 | tf_op jit(solution)/shard_map/all_to_all | solution.py:45
  267.5 140.1 %copy-start.3 = (bf16[256,1024]{1,0:T(8,128)(2,1)S(1)}, bf16[256,1024]{1,0:T(8,128)(2,1)}, u32[]{:S(2)}) copy-start(bf16[256,1024]{1,0:T(8,128)(2,1)} %param.15) | copy-start | bytes 1572868
  267.5 200.5 %reduce-scatter.2.cloned.1.call-start = ((), (), s32[]{:S(2)}) async-start(), calls=%async_computation.8 | async-start | bytes 2359296 | tf_op jit(solution)/shard_map/reduce_scatter | solution.py:83
  279.5 151.9 %copy-start.4 = (bf16[128]{0:T(256)(128)(2,1)S(1)}, bf16[128]{0:T(256)(128)(2,1)}, u32[]{:S(2)}) copy-start(bf16[128]{0:T(256)(128)(2,1)} %param.21) | copy-start | bytes 772
  279.5 151.9 %copy-start.5 = (bf16[128]{0:T(256)(128)(2,1)S(1)}, bf16[128]{0:T(256)(128)(2,1)}, u32[]{:S(2)}) copy-start(bf16[128]{0:T(256)(128)(2,1)} %param.20) | copy-start | bytes 772
  413.9 56.7 %copy-start = (bf16[256,1024]{1,0:T(8,128)(2,1)}, bf16[256,1024]{1,0:T(8,128)(2,1)S(1)}, u32[]{:S(2)}) copy-start(bf16[256,1024]{1,0:T(8,128)(2,1)S(1)} %fusion.39) | copy-start | bytes 1572868
Sparse Core Ops, SparseCore 0:
  10.6 79.5 all-gather.7
  92.8 75.0 all-gather.5
  169.8 51.9 all-gather.3
  431.6 36.4 reduce-scatter.1
where the time goes:
time: 478 us; the launch traced here: 477 us
  waiting for transfers between devices  345 us (72%)
  matrix products  43.1 us (9%)
  blocking collectives  32.6 us (7%)
  starting transfers between devices  16.1 us (3%)
  other arithmetic  15.2 us (3%)
  between operations  13.9 us (3%)
  local copies, waits for them, and re-layouts  11.3 us (2%)
    all_to_all x1, waiting for transfers between devices, on_device(): lax.all_to_all(send_rows, 'seq', split_axis=0, concat_axis=0, tiled=True)  128 us
    all_gather x1, waiting for transfers between devices, on_device(): lax.all_gather(key_weight, 'seq', axis=0, tiled=True)  72.8 us
    all_gather x1, waiting for transfers between devices, on_device(): lax.all_gather(value_weight, 'seq', axis=0, tiled=True)  55.9 us
    all_gather x1, waiting for transfers between devices, on_device(): lax.all_gather(patch_hidden, 'mp', axis=1, tiled=True).astype(jnp.float32)  49.5 us
    reduce_scatter x1, waiting for transfers between devices, on_device(): lax.psum_scatter(lax.dot_general(joined, normed, (((0,), (1,)), ((), ()))...  36.5 us
    dot_general x1, matrix products, on_device(): jnp.dot(activated, out_weight, preferred_element_type=jnp.float32)  31.9 us
    all_to_all x1, blocking collectives, on_device(): lax.all_to_all(send_slots, 'seq', split_axis=0, concat_axis=0, tiled=True)  20.1 us
    psum x1, blocking collectives, on_device(): squares = lax.psum(jnp.sum(stored * stored, axis=1), 'mp')  12.4 us
  transfers between devices with their start and end apart: 7, of which 5 were waited for; matrix products, arithmetic and copies ran while one was open for 12% of the time, Pallas kernels for 0%

commit v1 on v0

--- a/solution.py
+++ b/solution.py
@@ -35,7 +35,9 @@
         jnp.full((seq_count * capacity,), -1, jnp.int32).at[target].set(cluster_ids % slot_local)
     )
     activated = jax.nn.gelu(
-        lax.all_gather(patch_hidden, "mp", axis=1, tiled=True).astype(jnp.float32),
+        jnp.concatenate(
+            lax.all_to_all(jnp.stack([patch_hidden] * lax.axis_size("mp")), "mp", 0, 0), axis=1
+        ).astype(jnp.float32),
         approximate=False,
     ).astype(jnp.bfloat16)
     projected = jnp.dot(activated, out_weight, preferred_element_type=jnp.float32)

time: 478 us -> 430 us (0.90)
  waiting for transfers between devices: 345 us -> 282 us
  other arithmetic: 15.2 us -> 50.3 us
  matrix products: 43.1 us -> 21.1 us
  blocking collectives: 32.6 us -> 13.8 us
  starting transfers between devices: 16.1 us -> 31.7 us
    all_gather x1 -> x0, waiting for transfers between devices: 49.5 us -> none  [on_device(): lax.all_gather(patch_hidden, 'mp', axis=1, tiled=True).astype(jnp.float32)]
    all_gather x1, waiting for transfers between devices: 72.8 us -> 48.4 us  [on_device(): lax.all_gather(key_weight, 'seq', axis=0, tiled=True)]
    convert_element_type x0 -> x1, other arithmetic: none -> 23.4 us  [on_device(): activated = jax.nn.gelu(jnp.concatenate(lax.all_to_all(jnp.stack([patch_h...]
    dot_general x1, matrix products: 31.9 us -> 9.88 us  [on_device(): jnp.dot(activated, out_weight, preferred_element_type=jnp.float32)]
    all_to_all x1 -> x0, blocking collectives: 20.1 us -> none  [on_device(): lax.all_to_all(send_slots, 'seq', split_axis=0, concat_axis=0, tiled=True)]
    all_to_all x0 -> x2, waiting for transfers between devices: none -> 19 us  [the longest x1 11.8 us: on_device(): lax.all_to_all(jnp.stack([patch_hidden] * lax.axis_size('mp')), 'mp', 0, 0)]
    all_to_all x0 -> x2, starting transfers between devices: none -> 16.4 us  [the longest x1 11.7 us: on_device(): lax.all_to_all(send_slots, 'seq', split_axis=0, concat_axis=0, tiled=True)]
    mul x0 -> x1, other arithmetic: none -> 12.4 us  [on_device(): jax.nn.gelu(jnp.concatenate(lax.all_to_all(jnp.stack([patch_hidden] * lax...]
  transfers between devices with their start and end apart: 7 -> 8, of which waited for: 5 -> 6; matrix products, arithmetic and copies ran while one was open for 12% -> 17% of each run, Pallas kernels for 0% -> 0%
where the time goes in v1:
time: 430 us; the launch traced here: 429 us
  waiting for transfers between devices  282 us (66%)
  other arithmetic  50.3 us (12%)
  starting transfers between devices  31.7 us (7%)
  matrix products  21.1 us (5%)
  local copies, waits for them, and re-layouts  16 us (4%)
  between operations  14 us (3%)
  blocking collectives  13.8 us (3%)
    all_to_all x1, waiting for transfers between devices, on_device(): lax.all_to_all(send_rows, 'seq', split_axis=0, concat_axis=0, tiled=True)  128 us
    all_gather x1, waiting for transfers between devices, on_device(): lax.all_gather(value_weight, 'seq', axis=0, tiled=True)  50.1 us
    all_gather x1, waiting for transfers between devices, on_device(): lax.all_gather(key_weight, 'seq', axis=0, tiled=True)  48.4 us
    reduce_scatter x1, waiting for transfers between devices, on_device(): lax.psum_scatter(lax.dot_general(joined, normed, (((0,), (1,)), ((), ()))...  35 us
    convert_element_type x1, other arithmetic, on_device(): activated = jax.nn.gelu(jnp.concatenate(lax.all_to_all(jnp.stack([patch_h...  23.4 us
    psum x1, blocking collectives, on_device(): squares = lax.psum(jnp.sum(stored * stored, axis=1), 'mp')  13.8 us
    mul x1, other arithmetic, on_device(): jax.nn.gelu(jnp.concatenate(lax.all_to_all(jnp.stack([patch_hidden] * lax...  12.4 us
    all_to_all x1, waiting for transfers between devices, on_device(): lax.all_to_all(jnp.stack([patch_hidden] * lax.axis_size('mp')), 'mp', 0, 0)  11.8 us
  transfers between devices with their start and end apart: 8, of which 6 were waited for; matrix products, arithmetic and copies ran while one was open for 17% of the time, Pallas kernels for 0%

profile of v1, /device:TPU:8, one launch (start us, length us, event | category | flops | bytes accessed | tf_op | source)
XLA Modules:
  0.0 429.2 jit_solution(16560074326833328561)
XLA Ops:
  7.2 0.0 all-gather.3.cloned.1.call-start
  7.2 0.7 all-gather.3.cloned.1.call-update
  7.9 0.7 add_select_fusion
  8.6 1.2 reduce-window.6
  9.8 0.2 slice_reduce_fusion
  10.0 0.1 fusion.37
  10.2 2.5 scatter_custom_fusion
  12.6 0.7 all_to_all.41
  13.3 11.7 %all-to-all-start = ((s32[32,48,1]{1,2,0:T(1,128)}), s32[32,48,1]{1,2,0:T(1,128)S(1)}, u32[]{:S(2)}, u32[]{:S(2)}) async-start(s32[32,48,1]{1,2,0:T(1,128)} %bitcast.2), calls=%async_computation | async-start | bytes 32768 | tf_op jit(solution)/shard_map/all_to_all | solution.py:48
  25.0 1.3 copy.33
  26.4 0.0 copy-start.2
  26.4 7.2 %all-to-all-done = s32[32,48,1]{1,2,0:T(1,128)S(1)} async-done(((s32[32,48,1]{1,2,0:T(1,128)}), s32[32,48,1]{1,2,0:T(1,128)S(1)}, u32[]{:S(2)}, u32[]{:S(2)}) %all-to-all-start) | async-done | bytes 6176 | tf_op jit(solution)/shard_map/all_to_all | solution.py:48
  33.5 2.8 stack.4
  36.3 4.7 %all-to-all-start.1 = ((bf16[8,512,640]{1,2,0:T(8,128)(2,1)}), bf16[8,512,640]{1,2,0:T(8,128)(2,1)}, u32[]{:S(2)}, u32[]{:S(2)}) async-start(bf16[8,512,640]{1,2,0:T(8,128)(2,1)} %stack.4), calls=%async_computation.1 | async-start | bytes 10485760 | tf_op jit(solution)/shard_map/all_to_all | solution.py:39
  41.0 0.0 all-gather.5.cloned.1.call-start
  41.0 0.7 all-gather.5.cloned.1.call-update
  41.7 48.4 %all-gather.3.cloned.1.call-done = bf16[8192,128]{1,0:T(8,128)(2,1)} async-done(((bf16[256,128]{1,0:T(8,128)(2,1)}), bf16[8192,128]{1,0:T(8,128)(2,1)}) %all-gather.3.cloned.1.call-update) | async-done | bytes 2097168 | tf_op jit(solution)/shard_map/all_gather | solution.py:63
  90.1 11.8 %all-to-all-done.1 = bf16[8,512,640]{1,2,0:T(8,128)(2,1)} async-done(((bf16[8,512,640]{1,2,0:T(8,128)(2,1)}), bf16[8,512,640]{1,2,0:T(8,128)(2,1)}, u32[]{:S(2)}, u32[]{:S(2)}) %all-to-all-start.1) | async-done | bytes 5242912 | tf_op jit(solution)/shard_map/all_to_all | solution.py:39
  101.9 3.6 all-to-all-start.3
  105.5 0.0 copy-done.2
  105.5 12.4 %fusion = (f32[8,512,640]{1,2,0:T(8,128)}, f32[8,512,640]{1,2,0:T(8,128)}) fusion(bf16[8,512,640]{1,2,0:T(8,128)(2,1)} %all-to-all-done.1), kind=kLoop, calls=%fused_computation.5 | loop fusion | flops 10485760 | bytes 26214400 | tf_op jit(solution)/shard_map/mul | solution.py:37
  117.9 50.1 %all-gather.5.cloned.1.call-done = bf16[8192,128]{1,0:T(8,128)(2,1)} async-done(((bf16[256,128]{1,0:T(8,128)(2,1)}), bf16[8192,128]{1,0:T(8,128)(2,1)}) %all-gather.5.cloned.1.call-update) | async-done | bytes 2097168 | tf_op jit(solution)/shard_map/all_gather | solution.py:64
  168.0 0.0 all-to-all-done.3
  168.0 4.3 %all-to-all-start.4 = ((bf16[8,1024,128]{2,1,0:T(8,128)(2,1)}), bf16[8,1024,128]{2,1,0:T(8,128)(2,1)}, u32[]{:S(2)}, u32[]{:S(2)}) async-start(bf16[8,1024,128]{2,1,0:T(8,128)(2,1)} %bitcast.101), calls=%async_computation.4 | async-start | bytes 4194304 | tf_op jit(solution)/shard_map/all_to_all | solution.py:75
  172.3 23.4 %fusion.3 = bf16[512,5120]{0,1:T(8,128)(2,1)S(1)} fusion(f32[8,512,640]{1,2,0:T(8,128)} %get-tuple-element.19, f32[8,512,640]{1,2,0:T(8,128)} %get-tuple-element.18), kind=kLoop, calls=%fused_computation.8 | loop fusion | flops 162529280 | bytes 26214400 | tf_op jit(solution)/shard_map/convert_element_type | solution.py:42
  195.7 9.9 %fusion.42 = f32[512,1024]{1,0:T(8,128)} fusion(bf16[512,5120]{0,1:T(8,128)(2,1)S(1)} %fusion.3, bf16[5120,1024]{1,0:T(8,128)(2,1)} %param.12), kind=kOutput, calls=%fused_computation.72 | convolution fusion | flops 5368709120 | bytes 17825792 | tf_op jit(solution)/shard_map/dot_general | solution.py:43
  205.6 0.0 copy-start.1
  205.6 0.0 copy-start.3
  205.6 6.4 %scatter_custom_fusion.1 = f32[1536,1024]{1,0:T(8,128)} fusion(s32[512]{0:T(512)S(1)} %compare_select_fusion, f32[]{:T(128)} %constant.48.clone.1, f32[512,1024]{1,0:T(8,128)} %fusion.42, f32[1024]{0:T(1024)S(1)} %convert_element_type.55), kind=kCustom, calls=%fused_computation.28 | custom fusion | flops 524288 | bytes 8392708 | tf_op jit(solution)/shard_map/scatter | solution.py:45
  212.0 0.0 all-to-all-done.4
  212.0 7.3 %all-to-all-start.2 = ((f32[32,48,1024]{2,1,0:T(8,128)}), f32[32,48,1024]{2,1,0:T(8,128)}, u32[]{:S(2)}, u32[]{:S(2)}) async-start(f32[32,48,1024]{2,1,0:T(8,128)} %bitcast.97), calls=%async_computation.2 | async-start | bytes 12582912 | tf_op jit(solution)/shard_map/all_to_all | solution.py:47
  219.4 0.0 copy-start.4
  219.4 0.0 reduce-scatter.2.cloned.1.call-start
  219.4 0.0 copy-done.1
  219.5 0.0 copy-done.3
  219.5 0.5 broadcast.83
  220.0 0.7 reduce.5
  220.7 0.1 eq.48
  220.8 0.2 convert_reduce_fusion
  221.0 3.9 pad_maximum_fusion
  224.9 6.5 %copy.34 = bf16[1024,8,2,128]{0,3,2,1:T(8,128)(2,1)} copy(bf16[1024,8,2,128]{3,0,1,2:T(8,128)(2,1)} %pad_maximum_fusion) | data formatting | bytes 8388608 | tf_op jit(solution)/shard_map/stack | solution.py:78
  231.4 0.0 copy-start.5
  231.4 0.0 copy-start.6
  231.4 128.4 %all-to-all-done.2 = f32[32,48,1024]{2,1,0:T(8,128)} async-done(((f32[32,48,1024]{2,1,0:T(8,128)}), f32[32,48,1024]{2,1,0:T(8,128)}, u32[]{:S(2)}, u32[]{:S(2)}) %all-to-all-start.2) | async-done | bytes 6291488 | tf_op jit(solution)/shard_map/all_to_all | solution.py:47
  359.7 0.0 copy-done.4
  359.7 6.3 %fusion.24 = bf16[256,1024]{1,0:T(8,128)(2,1)S(1)} fusion(f32[1536,1024]{1,0:T(8,128)} %bitcast.9, bf16[256,1024]{1,0:T(8,128)(2,1)S(1)} %copy-done.4, s32[1536]{0:T(1024)S(1)} %eq.48, f32[256]{0:T(256)S(1)} %convert_add_fusion, f32[256]{0:T(256)S(1)} %convert_element_type.50), kind=kOutput, calls=%fused_computation.38 | convolution fusion | flops 4833542144 | bytes 7348224 | tf_op jit(solution)/shard_map/dot_general | solution.py:51
  366.0 0.0 copy-start
  366.0 0.2 fusion.25
  366.2 13.8 %psum.7 = f32[256]{0:T(256)S(1)} all-reduce(f32[256]{0:T(256)S(1)} %fusion.25), channel_id=1, replica_groups=mesh['seq'=32,'mp'=8] {'mp'}, use_global_device_ids=true, to_apply=%region_7.8 | all-reduce | flops 256 | bytes 2048 | tf_op jit(solution)/shard_map/psum | solution.py:68
  380.1 4.9 %fusion.30 = f32[2048,256]{1,0:T(8,128)} fusion(bf16[1024,2048]{0,1:T(8,128)(2,1)} %bitcast.99, bf16[256,1024]{1,0:T(8,128)(2,1)S(1)} %fusion.24, f32[1024]{0:T(1024)S(1)} %convert_element_type.59, f32[256]{0:T(256)S(1)} %add_rsqrt_fusion), kind=kOutput, calls=%fused_computation.44 | convolution fusion | flops 1074790400 | bytes 6820864 | tf_op jit(solution)/shard_map/dot_general | solution.py:86
  385.0 0.0 reduce-scatter.2.cloned.1.call-update
  385.0 0.0 copy-done.5
  385.0 0.0 copy-done.6
  385.1 35.0 %reduce-scatter.2.cloned.1.call-done = f32[256,256]{1,0:T(8,128)} async-done(((f32[2048,256]{1,0:T(8,128)}), f32[256,256]{1,0:T(8,128)}) %reduce-scatter.2.cloned.1.call-update) | async-done | bytes 262160 | tf_op jit(solution)/shard_map/reduce_scatter | solution.py:85
  420.1 1.1 fusion.34
  421.2 0.7 copy.35
  421.9 0.7 copy.36
  422.6 0.0 copy-done
  (11 shorter events, 0.1 us)
Async XLA Ops:
  7.2 82.9 %all-gather.3.cloned.1.call-start = ((), (), s32[]{:S(2)}) async-start(), calls=%async_computation.6 | async-start | bytes 2162688 | tf_op jit(solution)/shard_map/all_gather | solution.py:63
  13.3 20.2 %all-to-all-start = ((s32[32,48,1]{1,2,0:T(1,128)}), s32[32,48,1]{1,2,0:T(1,128)S(1)}, u32[]{:S(2)}, u32[]{:S(2)}) async-start(s32[32,48,1]{1,2,0:T(1,128)} %bitcast.2), calls=%async_computation | async-start | bytes 32768 | tf_op jit(solution)/shard_map/all_to_all | solution.py:48
  26.4 79.1 %copy-start.2 = (bf16[1024]{0:T(1024)(128)(2,1)S(1)}, bf16[1024]{0:T(1024)(128)(2,1)}, u32[]{:S(2)}) copy-start(bf16[1024]{0:T(1024)(128)(2,1)} %param.13) | copy-start | bytes 6148
  36.3 65.6 %all-to-all-start.1 = ((bf16[8,512,640]{1,2,0:T(8,128)(2,1)}), bf16[8,512,640]{1,2,0:T(8,128)(2,1)}, u32[]{:S(2)}, u32[]{:S(2)}) async-start(bf16[8,512,640]{1,2,0:T(8,128)(2,1)} %stack.4), calls=%async_computation.1 | async-start | bytes 10485760 | tf_op jit(solution)/shard_map/all_to_all | solution.py:39
  41.0 127.0 %all-gather.5.cloned.1.call-start = ((), (), s32[]{:S(2)}) async-start(), calls=%async_computation.7 | async-start | bytes 2162688 | tf_op jit(solution)/shard_map/all_gather | solution.py:64
  101.9 66.1 %all-to-all-start.3 = ((bf16[8,1024,128]{2,1,0:T(8,128)(2,1)}), bf16[8,1024,128]{2,1,0:T(8,128)(2,1)S(1)}, u32[]{:S(2)}, u32[]{:S(2)}) async-start(bf16[8,1024,128]{2,1,0:T(8,128)(2,1)} %bitcast.100), calls=%async_computation.3 | async-start | bytes 4194304 | tf_op jit(solution)/shard_map/all_to_all | solution.py:74
  168.0 44.1 %all-to-all-start.4 = ((bf16[8,1024,128]{2,1,0:T(8,128)(2,1)}), bf16[8,1024,128]{2,1,0:T(8,128)(2,1)}, u32[]{:S(2)}, u32[]{:S(2)}) async-start(bf16[8,1024,128]{2,1,0:T(8,128)(2,1)} %bitcast.101), calls=%async_computation.4 | async-start | bytes 4194304 | tf_op jit(solution)/shard_map/all_to_all | solution.py:75
  205.6 13.8 %copy-start.1 = (s32[256]{0:T(256)S(1)}, s32[256]{0:T(256)}, u32[]{:S(2)}) copy-start(s32[256]{0:T(256)} %param.16) | copy-start | bytes 3076
  205.6 13.9 %copy-start.3 = (bf16[1024]{0:T(1024)(128)(2,1)S(1)}, bf16[1024]{0:T(1024)(128)(2,1)}, u32[]{:S(2)}) copy-start(bf16[1024]{0:T(1024)(128)(2,1)} %param.17) | copy-start | bytes 6148
  212.0 147.7 %all-to-all-start.2 = ((f32[32,48,1024]{2,1,0:T(8,128)}), f32[32,48,1024]{2,1,0:T(8,128)}, u32[]{:S(2)}, u32[]{:S(2)}) async-start(f32[32,48,1024]{2,1,0:T(8,128)} %bitcast.97), calls=%async_computation.2 | async-start | bytes 12582912 | tf_op jit(solution)/shard_map/all_to_all | solution.py:47
  219.4 140.4 %copy-start.4 = (bf16[256,1024]{1,0:T(8,128)(2,1)S(1)}, bf16[256,1024]{1,0:T(8,128)(2,1)}, u32[]{:S(2)}) copy-start(bf16[256,1024]{1,0:T(8,128)(2,1)} %param.15) | copy-start | bytes 1572868
  219.4 200.7 %reduce-scatter.2.cloned.1.call-start = ((), (), s32[]{:S(2)}) async-start(), calls=%async_computation.8 | async-start | bytes 2359296 | tf_op jit(solution)/shard_map/reduce_scatter | solution.py:85
  231.4 153.6 %copy-start.5 = (bf16[128]{0:T(256)(128)(2,1)S(1)}, bf16[128]{0:T(256)(128)(2,1)}, u32[]{:S(2)}) copy-start(bf16[128]{0:T(256)(128)(2,1)} %param.20) | copy-start | bytes 772
  231.4 153.7 %copy-start.6 = (bf16[128]{0:T(256)(128)(2,1)S(1)}, bf16[128]{0:T(256)(128)(2,1)}, u32[]{:S(2)}) copy-start(bf16[128]{0:T(256)(128)(2,1)} %param.21) | copy-start | bytes 772
  366.0 56.6 %copy-start = (bf16[256,1024]{1,0:T(8,128)(2,1)}, bf16[256,1024]{1,0:T(8,128)(2,1)S(1)}, u32[]{:S(2)}) copy-start(bf16[256,1024]{1,0:T(8,128)(2,1)S(1)} %fusion.24) | copy-start | bytes 1572868
Sparse Core Ops, SparseCore 0:
  10.6 79.4 all-gather.2
  92.7 75.2 all-gather.4
  385.1 34.8 reduce-scatter.1
